TPU v7x, 256 devices: a whole 4x4x8 slice. The times are simulated.
256 devices in a mesh: nodes: 64 (over z, y, core), chaos: 4 (over x).
Axes of the slice: x: 4, y: 4, z: 8, core: 2. Of those that a mesh axis runs over, the one named last changes fastest.
Arguments:
- right_side: float32 [120, 262144], P('chaos', 'nodes'), may hold values from -6 to 6
- diag_blocks: float32 [4096, 4096], P('nodes')
- off_blocks: float32 [4096, 4, 4096], P('nodes'), may hold values from -3 to 3
- smoother: float32 [4096, 4096], P('nodes')
- col_index: int32 [4096, 4], P('nodes'), may hold values from 0 to 79
- send_list: int32 [1024], P('nodes'), may hold values from 0 to 63
- agg_map: int32 [262144], P('nodes'), may hold values from 0 to 255
- owner_map: int32 [16384, 1], P('nodes'), may hold values from 0 to 15; in each aligned block of 256 rows (0 to 255, 256 to 511, ...) at most 20 rows name the same one
- coarse_diag: float32 [16384], P('nodes'), may hold values from 1 to 4
- coarse_weight: float32 [16384], P('nodes'), may hold values from 0.0001953125 to 0.001953125
- coarse_gain: float32 [16384], P('nodes'), may hold values from 0.2 to 2
Outputs:
- solution_field: float32 [120, 262144], P('chaos', 'nodes')
- residual_ratio: float32 [], replicated
Inputs may be any that keep to these rules, and one draw needn't show every extreme that they name: `owner_map`: no owner gets more than 20 aggregates of one device; on some device one owner gets exactly 20. `send_list`: the first 8 entries of a device are blocks its previous device reads, the last 8 those its next device reads.
All inputs are finite; a program needn't handle non-finite values.
Results may differ from a plain program's by a relative error of at most 0.0003.
Values sent between devices are 32-bit elements; how exact they have to be, the bound alone decides.
A program may use at most 128 MiB of HBM per device.

v0:
```python
import jax
import jax.numpy as jnp
from jax import lax
from jax.sharding import PartitionSpec as P

H = 8
CSWEEPS = 3
NA_DEV = 256


def extended_2(block, sides, width):
    for axis, dim in sides:
        count = lax.axis_size(axis)
        forward = [(i, i + 1) for i in range(count - 1)]
        forward.append((count - 1, 0))
        backward = [(target, source) for source, target in forward]
        low = lax.ppermute(
            lax.slice_in_dim(block, block.shape[dim] - width, None, axis=dim), axis, forward
        )
        high = lax.ppermute(lax.slice_in_dim(block, 0, width, axis=dim), axis, backward)
        block = jnp.concatenate([low, block, high], axis=dim)
    return block


def on_device(
    right_side,
    diag_blocks,
    off_blocks,
    smoother,
    col_index,
    send_list,
    agg_map,
    owner_map,
    coarse_diag,
    coarse_weight,
    coarse_gain,
):
    hi = lax.Precision.HIGHEST
    terms, width = right_side.shape
    nblk = width // 64
    count_nodes = lax.axis_size("nodes")
    owners = count_nodes // 4
    slots = min(NA_DEV, 4 * max(2, 5 * NA_DEV // (16 * owners)))
    quarter = slots // 4
    rim = H * 64
    diag_mats = diag_blocks.reshape(nblk, 64, 64)
    off_mats = off_blocks.reshape(nblk, off_blocks.shape[1], 64, 64)
    smooth_mats = smoother.reshape(nblk, 64, 64)

    def apply_op(field):
        blocks = field.reshape(terms, nblk, 64)
        export = blocks[:, send_list].reshape(terms, 2 * rim)
        padded = extended_2(export, (("nodes", 1),), rim)
        extended = jnp.concatenate([field, padded[:, :rim], padded[:, 3 * rim :]], 1).reshape(
            terms, nblk + 2 * H, 64
        )
        near = extended[:, col_index]
        own = jnp.einsum("bij,pbj->pbi", diag_mats, blocks, precision=hi)
        far = jnp.einsum("bkij,pbkj->pbi", off_mats, near, precision=hi)
        return (own + far).reshape(terms, width)

    def smooth(field):
        return jnp.einsum(
            "bij,pbj->pbi", smooth_mats, field.reshape(terms, nblk, 64), precision=hi
        ).reshape(terms, width)

    first = smooth(right_side)
    second = first + smooth(right_side - apply_op(first))
    resid = right_side - apply_op(second)
    coarse_res = jax.ops.segment_sum(resid.T, agg_map, num_segments=NA_DEV).T
    owner = owner_map[:, 0]
    onehot = (owner[:, None] == jnp.arange(owners, dtype=jnp.int32)[None, :]).astype(jnp.float32)
    before = jnp.cumsum(onehot, 0) - onehot
    slot = jnp.sum(before * onehot, 1).astype(jnp.int32)
    target = (owner * 4 + slot % 4) * quarter + slot // 4
    packed_res = (
        jnp.zeros((count_nodes * quarter, terms), jnp.float32)
        .at[target]
        .set(coarse_res.T)
        .reshape(count_nodes, quarter, terms)
    )
    flat = jnp.zeros((count_nodes * quarter,), jnp.float32)
    packed_diag = flat.at[target].set(coarse_diag).reshape(count_nodes, quarter)
    packed_weight = flat.at[target].set(coarse_weight).reshape(count_nodes, quarter)
    packed_gain = flat.at[target].set(coarse_gain).reshape(count_nodes, quarter)
    got_res, got_diag, got_weight, got_gain = (
        lax.all_to_all(packed_res, "nodes", split_axis=0, concat_axis=0, tiled=True),
        lax.all_to_all(packed_diag, "nodes", split_axis=0, concat_axis=0, tiled=True),
        lax.all_to_all(packed_weight, "nodes", split_axis=0, concat_axis=0, tiled=True),
        lax.all_to_all(packed_gain, "nodes", split_axis=0, concat_axis=0, tiled=True),
    )
    live = got_diag > 0.0
    safe = jnp.where(live, got_diag, 1.0)[..., None]
    corr = jnp.where(live[..., None], got_res / safe, 0.0)
    my_owner = lax.axis_index("nodes") // 4
    select = (jnp.arange(owners, dtype=jnp.int32) == my_owner).astype(jnp.float32)
    for sweep in range(CSWEEPS - 1):
        local = jnp.sum(got_weight[..., None] * corr, (0, 1))
        group = lax.psum(local[:, None] * select[None, :], "nodes")
        total = jnp.sum(group * select[None, :], 1)
        corr = corr + (got_res - got_diag[..., None] * corr + got_gain[..., None] * total) / safe
    returned = lax.all_to_all(corr, "nodes", split_axis=0, concat_axis=0, tiled=True)
    coarse_corr = returned.reshape(count_nodes * quarter, terms)[target].T
    third = second + coarse_corr[:, agg_map]
    solution_field = third + smooth(right_side - apply_op(third))
    final = right_side - apply_op(solution_field)
    final_sq, right_sq = lax.psum(
        (jnp.sum(final * final), jnp.sum(right_side * right_side)), ("nodes", "chaos")
    )
    ratio = jnp.sqrt(final_sq / (right_sq + 1e-06))
    return (solution_field, ratio)


def solution(mesh):
    placed = (
        P("chaos", "nodes"),
        P("nodes", None),
        P("nodes", None, None),
        P("nodes", None),
        P("nodes", None),
        P("nodes"),
        P("nodes"),
        P("nodes", None),
        P("nodes"),
        P("nodes"),
        P("nodes"),
    )
    return jax.shard_map(
        on_device, mesh=mesh, in_specs=placed, out_specs=(P("chaos", "nodes"), P()), check_vma=False
    )
```

profile of v0, /device:TPU:1, one launch (start us, length us, event | category | flops | bytes accessed | tf_op | source)
XLA Modules:
  0.0 656.6 jit_solution(9537910008916404787)
XLA Ops:
  5.5 4.9 convolution_bitcast_fusion.6
  20.0 12.7 %all-to-all-start = ((f32[64,1,5]{2,1,0:T(1,128)}), f32[64,1,5]{2,1,0:T(1,128)S(1)}, u32[]{:S(2)}, u32[]{:S(2)}) async-start(f32[64,1,5]{2,1,0:T(1,128)} %bitcast.13), calls=%async_computation | async-start | bytes 65536 | tf_op jit(solution)/shard_map/all_to_all | solution.py:88
  43.2 8.1 %reshape.214 = f32[64,4,64,64]{3,2,1,0:T(8,128)} reshape(f32[64,4,4096]{2,1,0:T(4,128)} %param.13) | data formatting | bytes 8388608 | tf_op jit(solution)/shard_map/reshape | solution.py:47
  62.5 10.8 %fusion.4 = f32[30,64,64]{2,0,1:T(8,128)S(1)} fusion(f32[64,30,64]{2,1,0:T(8,128)} %fusion.33, f32[30,64,4,64]{3,0,2,1:T(8,128)} %bitcast.113, f32[64,4,64,64]{3,2,1,0:T(8,128)} %reshape.214), kind=kOutput, calls=%fused_computation.26 | convolution fusion | flops 377610240 | bytes 7143424 | tf_op jit(solution)/shard_map/bkij,pbkj->pbi/dot_general | solution.py:59
  81.8 6.9 %fusion.31 = (f32[30,64,64]{2,0,1:T(8,128)}, f32[30,64,64]{2,0,1:T(8,128)}) fusion(f32[30,64,64]{2,0,1:T(8,128)S(1)} %copy-done.2, f32[64,64,64]{2,1,0:T(8,128)} %copy-done, f32[30,64,64]{2,1,0:T(8,128)} %reshape.216), kind=kOutput, calls=%fused_computation.91 | convolution fusion | flops 94494720 | bytes 3014656 | tf_op jit(solution)/shard_map/bij,pbj->pbi/dot_general | solution.py:63
  92.5 11.5 %collective-permute-start.3 = (f32[30,512]{1,0:T(8,128)S(1)}, f32[30,512]{1,0:T(8,128)S(1)}, u32[]{:S(2)}, u32[]{:S(2)}) collective-permute-start(f32[30,512]{1,0:T(8,128)S(1)} %get-tuple-element.23), channel_id=1, source_target_pairs={{4,0},{8,4},{12,8},{16,12},{20,16},{24,20},{28,24},{32,28},{36,32}... | collective-permute-start | bytes 184328 | tf_op jit(solution)/shard_map/ppermute | solution.py:20
  104.0 5.6 fusion.34
  119.8 10.9 %fusion.5 = f32[30,64,64]{2,0,1:T(8,128)S(1)} fusion(f32[64,30,64]{2,1,0:T(8,128)} %fusion.34, f32[30,64,4,64]{3,0,2,1:T(8,128)} %bitcast.114, f32[64,4,64,64]{3,2,1,0:T(8,128)} %reshape.214), kind=kOutput, calls=%fused_computation.27 | convolution fusion | flops 377610240 | bytes 7143424 | tf_op jit(solution)/shard_map/bkij,pbkj->pbi/dot_general | solution.py:59
  137.8 22.7 %scatter_custom_fusion.1 = f32[256,30]{1,0:T(8,128)S(1)} fusion(s32[4096]{0:T(1024)S(1)} %copy-done.14, f32[4096,30]{1,0:T(8,128)} %copy.200, f32[]{:T(128)} %constant.59.clone.1), kind=kCustom, calls=%fused_computation.48 | custom fusion | flops 122880 | bytes 31232 | tf_op jit(solution)/shard_map/scatter-add | solution.py:70
  162.5 11.3 %all-to-all-start.1 = ((f32[64,1,150]{2,1,0:T(1,128)}), f32[64,1,150]{2,1,0:T(1,128)S(1)}, u32[]{:S(2)}, u32[]{:S(2)}) async-start(f32[64,1,150]{2,1,0:T(1,128)} %reshape.381), calls=%async_computation.1 | async-start | bytes 131072 | tf_op jit(solution)/shard_map/all_to_all | solution.py:87
  173.8 10.1 %all-to-all-done.1 = f32[64,1,150]{2,1,0:T(1,128)S(1)} async-done(((f32[64,1,150]{2,1,0:T(1,128)}), f32[64,1,150]{2,1,0:T(1,128)S(1)}, u32[]{:S(2)}, u32[]{:S(2)}) %all-to-all-start.1) | async-done | bytes 38432 | tf_op jit(solution)/shard_map/all_to_all | solution.py:87
  189.8 8.0 %all-to-all-done.3 = f32[64,1,5]{2,1,0:T(1,128)S(1)} async-done(((f32[64,1,5]{2,1,0:T(1,128)}), f32[64,1,5]{2,1,0:T(1,128)S(1)}, u32[]{:S(2)}, u32[]{:S(2)}) %all-to-all-start.3) | async-done | bytes 1312 | tf_op jit(solution)/shard_map/all_to_all | solution.py:89
  197.8 4.6 all-to-all-start.2
  202.8 126.6 %psum.28 = f32[30,16]{0,1:T(8,128)S(1)} all-reduce(f32[30,16]{0,1:T(8,128)S(1)} %broadcast_multiply_fusion.1), channel_id=1, replica_groups=mesh['nodes'=64,'chaos'=4] {'nodes'}, use_global_device_ids=true, to_apply=%region_9.10 | all-reduce | flops 480 | bytes 3840 | tf_op jit(solution)/shard_map/psum | solution.py:99
  330.1 130.8 %psum.29 = f32[30,16]{0,1:T(8,128)S(1)} all-reduce(f32[30,16]{0,1:T(8,128)S(1)} %broadcast_multiply_fusion), channel_id=1, replica_groups=mesh['nodes'=64,'chaos'=4] {'nodes'}, use_global_device_ids=true, to_apply=%region_12.13 | all-reduce | flops 480 | bytes 3840 | tf_op jit(solution)/shard_map/psum | solution.py:99
  462.1 5.6 all-to-all-start.4
  467.7 10.1 %all-to-all-done.4 = f32[64,1,150]{2,1,0:T(1,128)S(1)} async-done(((f32[64,1,150]{2,1,0:T(1,128)}), f32[64,1,150]{2,1,0:T(1,128)S(1)}, u32[]{:S(2)}, u32[]{:S(2)}) %all-to-all-start.4) | async-done | bytes 38432 | tf_op jit(solution)/shard_map/all_to_all | solution.py:102
  479.4 14.1 %gather_fusion.5 = f32[4096,30]{1,0:T(8,128)} fusion(f32[30,256]{0,1:T(8,128)S(1)} %bitcast.111, s32[4096]{0:T(1024)S(1)} %fusion.15), kind=kCustom, calls=%fused_computation.5 | custom fusion | bytes 999424 | tf_op jit(solution)/shard_map/gather | solution.py:104
  506.7 5.6 fusion.35
  518.5 11.0 %fusion.6 = f32[30,64,64]{2,0,1:T(8,128)S(1)} fusion(f32[64,30,64]{2,1,0:T(8,128)} %fusion.35, f32[30,64,4,64]{3,0,2,1:T(8,128)} %bitcast.115, f32[64,4,64,64]{3,2,1,0:T(8,128)} %reshape.214), kind=kOutput, calls=%fused_computation.28 | convolution fusion | flops 377610240 | bytes 7143424 | tf_op jit(solution)/shard_map/bkij,pbkj->pbi/dot_general | solution.py:59
  535.9 7.2 %fusion.32 = (f32[30,64,64]{2,0,1:T(8,128)}, f32[30,64,64]{2,0,1:T(8,128)}) fusion(f32[30,64,64]{2,0,1:T(8,128)} %copy_add_fusion, f32[64,64,64]{2,1,0:T(8,128)} %copy-done, f32[30,64,64]{2,1,0:T(8,128)} %reshape.227), kind=kOutput, calls=%fused_computation.92 | convolution fusion | flops 94494720 | bytes 3014656 | tf_op jit(solution)/shard_map/bij,pbj->pbi/dot_general | solution.py:63
  550.5 5.6 fusion.36
  563.4 10.7 %fusion.7 = f32[30,64,64]{2,0,1:T(8,128)S(1)} fusion(f32[64,30,64]{2,1,0:T(8,128)} %fusion.36, f32[30,64,4,64]{3,0,2,1:T(8,128)} %bitcast.112, f32[64,4,64,64]{3,2,1,0:T(8,128)} %reshape.214), kind=kOutput, calls=%fused_computation.29 | convolution fusion | flops 377610240 | bytes 7143424 | tf_op jit(solution)/shard_map/bkij,pbkj->pbi/dot_general | solution.py:59
  575.9 78.1 %all-reduce = (f32[]{:T(128)}, f32[]{:T(128)}) all-reduce(f32[]{:T(128)} %get-tuple-element.15, f32[]{:T(128)} %get-tuple-element.14), channel_id=1, replica_groups=mesh['nodes'=64,'chaos'=4] {'nodes','chaos'}, use_global_device_ids=true, to_apply=%region_15.16 | all-reduce | flops 2 | bytes 16 | tf_op jit(solution)/shard_map/psum | solution.py:107
  (160 shorter events, 119.4 us)
Async XLA Ops:
  2.7 31.6 %copy-start = (f32[64,64,64]{2,1,0:T(8,128)}, f32[64,64,64]{2,1,0:T(8,128)S(1)}, u32[]{:S(2)}) copy-start(f32[64,64,64]{2,1,0:T(8,128)S(1)} %reshape.209) | copy-start | bytes 3145732
  2.7 14.1 %copy-start.15 = (s32[256,1]{0,1:T(1,128)S(1)}, s32[256,1]{0,1:T(1,128)}, u32[]{:S(2)}) copy-start(s32[256,1]{0,1:T(1,128)} %param.18) | copy-start | bytes 3076
  5.5 31.0 %copy-start.16 = (s32[64,4]{0,1:T(4,128)S(1)}, s32[64,4]{0,1:T(4,128)}, u32[]{:S(2)}) copy-start(s32[64,4]{0,1:T(4,128)} %param.15) | copy-start | bytes 3076
  10.4 28.4 %copy-start.1 = (f32[30,64,64]{2,0,1:T(8,128)}, f32[30,64,64]{2,0,1:T(8,128)S(1)}, u32[]{:S(2)}) copy-start(f32[30,64,64]{2,0,1:T(8,128)S(1)} %convolution_bitcast_fusion.6) | copy-start | bytes 1474564
  13.5 42.7 %collective-permute-start = (f32[30,512]{1,0:T(8,128)}, f32[30,512]{1,0:T(8,128)S(1)}, u32[]{:S(2)}, u32[]{:S(2)}) collective-permute-start(f32[30,512]{1,0:T(8,128)} %get-tuple-element.24), channel_id=1, source_target_pairs={{0,4},{4,8},{8,12},{12,16},{16,20},{20,24},{24,28},{28,32},{32,36}... | collective-permute-start | bytes 184328 | tf_op jit(solution)/shard_map/ppermute | solution.py:17
  16.2 40.1 %collective-permute-start.1 = (f32[30,512]{1,0:T(8,128)S(1)}, f32[30,512]{1,0:T(8,128)S(1)}, u32[]{:S(2)}, u32[]{:S(2)}) collective-permute-start(f32[30,512]{1,0:T(8,128)S(1)} %get-tuple-element.25), channel_id=1, source_target_pairs={{4,0},{8,4},{12,8},{16,12},{20,16},{24,20},{28,24},{32,28},{36,32}... | collective-permute-start | bytes 184328 | tf_op jit(solution)/shard_map/ppermute | solution.py:20
  20.0 142.5 %all-to-all-start = ((f32[64,1,5]{2,1,0:T(1,128)}), f32[64,1,5]{2,1,0:T(1,128)S(1)}, u32[]{:S(2)}, u32[]{:S(2)}) async-start(f32[64,1,5]{2,1,0:T(1,128)} %bitcast.13), calls=%async_computation | async-start | bytes 65536 | tf_op jit(solution)/shard_map/all_to_all | solution.py:88
  43.2 13.1 %copy-start.14 = (s32[4096]{0:T(1024)S(1)}, s32[4096]{0:T(1024)}, u32[]{:S(2)}) copy-start(s32[4096]{0:T(1024)} %param.17) | copy-start | bytes 49156
  43.2 13.1 %copy-start.7 = (f32[30,4096]{1,0:T(8,128)S(1)}, f32[30,4096]{1,0:T(8,128)}, u32[]{:S(2)}) copy-start(f32[30,4096]{1,0:T(8,128)} %reshape.210) | copy-start | bytes 1474564
  90.8 18.8 %copy-start.12 = (f32[30,64,64]{2,0,1:T(8,128)S(1)}, f32[30,64,64]{2,0,1:T(8,128)}, u32[]{:S(2)}) copy-start(f32[30,64,64]{2,0,1:T(8,128)} %get-tuple-element.27) | copy-start | bytes 1474564
  90.8 21.9 %copy-start.8 = (f32[30,4096]{1,0:T(8,128)S(1)}, f32[30,4096]{1,0:T(8,128)}, u32[]{:S(2)}) copy-start(f32[30,4096]{1,0:T(8,128)} %reshape.210) | copy-start | bytes 1474564
  90.8 22.0 %collective-permute-start.2 = (f32[30,512]{1,0:T(8,128)S(1)}, f32[30,512]{1,0:T(8,128)S(1)}, u32[]{:S(2)}, u32[]{:S(2)}) collective-permute-start(f32[30,512]{1,0:T(8,128)S(1)} %get-tuple-element.22), channel_id=1, source_target_pairs={{0,4},{4,8},{8,12},{12,16},{16,20},{20,24},{24,28},{28,32},{32,36}... | collective-permute-start | bytes 184328 | tf_op jit(solution)/shard_map/ppermute | solution.py:17
  92.5 20.3 %collective-permute-start.3 = (f32[30,512]{1,0:T(8,128)S(1)}, f32[30,512]{1,0:T(8,128)S(1)}, u32[]{:S(2)}, u32[]{:S(2)}) collective-permute-start(f32[30,512]{1,0:T(8,128)S(1)} %get-tuple-element.23), channel_id=1, source_target_pairs={{4,0},{8,4},{12,8},{16,12},{20,16},{24,20},{28,24},{32,28},{36,32}... | collective-permute-start | bytes 184328 | tf_op jit(solution)/shard_map/ppermute | solution.py:20
  119.8 14.0 %copy-start.3 = (f32[30,4096]{1,0:T(8,128)S(1)}, f32[30,4096]{1,0:T(8,128)}, u32[]{:S(2)}) copy-start(f32[30,4096]{1,0:T(8,128)} %param.11) | copy-start | bytes 1474564
  162.5 21.4 %all-to-all-start.1 = ((f32[64,1,150]{2,1,0:T(1,128)}), f32[64,1,150]{2,1,0:T(1,128)S(1)}, u32[]{:S(2)}, u32[]{:S(2)}) async-start(f32[64,1,150]{2,1,0:T(1,128)} %reshape.381), calls=%async_computation.1 | async-start | bytes 131072 | tf_op jit(solution)/shard_map/all_to_all | solution.py:87
  183.9 13.9 %all-to-all-start.3 = ((f32[64,1,5]{2,1,0:T(1,128)}), f32[64,1,5]{2,1,0:T(1,128)S(1)}, u32[]{:S(2)}, u32[]{:S(2)}) async-start(f32[64,1,5]{2,1,0:T(1,128)} %bitcast.24), calls=%async_computation.3 | async-start | bytes 65536 | tf_op jit(solution)/shard_map/all_to_all | solution.py:89
  197.8 131.7 %all-to-all-start.2 = ((f32[64,1,5]{2,1,0:T(1,128)}), f32[64,1,5]{2,1,0:T(1,128)S(1)}, u32[]{:S(2)}, u32[]{:S(2)}) async-start(f32[64,1,5]{2,1,0:T(1,128)} %bitcast.22), calls=%async_computation.2 | async-start | bytes 65536 | tf_op jit(solution)/shard_map/all_to_all | solution.py:90
  462.1 15.7 %all-to-all-start.4 = ((f32[64,1,150]{2,1,0:T(1,128)}), f32[64,1,150]{2,1,0:T(1,128)S(1)}, u32[]{:S(2)}, u32[]{:S(2)}) async-start(f32[64,1,150]{2,1,0:T(1,128)} %reshape.383), calls=%async_computation.4 | async-start | bytes 131072 | tf_op jit(solution)/shard_map/all_to_all | solution.py:102
  506.1 6.2 collective-permute-start.4
  506.6 5.6 collective-permute-start.5
  518.5 14.1 %copy-start.4 = (f32[30,4096]{1,0:T(8,128)S(1)}, f32[30,4096]{1,0:T(8,128)}, u32[]{:S(2)}) copy-start(f32[30,4096]{1,0:T(8,128)} %param.11) | copy-start | bytes 1474564
  545.2 11.9 %copy-start.10 = (f32[30,4096]{1,0:T(8,128)S(1)}, f32[30,4096]{1,0:T(8,128)}, u32[]{:S(2)}) copy-start(f32[30,4096]{1,0:T(8,128)} %bitcast_add_fusion) | copy-start | bytes 1474564
  545.2 12.0 %collective-permute-start.6 = (f32[30,512]{1,0:T(8,128)S(1)}, f32[30,512]{1,0:T(8,128)S(1)}, u32[]{:S(2)}, u32[]{:S(2)}) collective-permute-start(f32[30,512]{1,0:T(8,128)S(1)} %get-tuple-element.18), channel_id=1, source_target_pairs={{0,4},{4,8},{8,12},{12,16},{16,20},{20,24},{24,28},{28,32},{32,36}... | collective-permute-start | bytes 184328 | tf_op jit(solution)/shard_map/ppermute | solution.py:17
  547.0 10.2 %collective-permute-start.7 = (f32[30,512]{1,0:T(8,128)S(1)}, f32[30,512]{1,0:T(8,128)S(1)}, u32[]{:S(2)}, u32[]{:S(2)}) collective-permute-start(f32[30,512]{1,0:T(8,128)S(1)} %get-tuple-element.19), channel_id=1, source_target_pairs={{4,0},{8,4},{12,8},{16,12},{20,16},{24,20},{28,24},{32,28},{36,32}... | collective-permute-start | bytes 184328 | tf_op jit(solution)/shard_map/ppermute | solution.py:20
  (7 other events, 47.4 us)
where the time goes:
time: 659 us; the launch traced here: 657 us
  blocking collectives  335 us (51%)
  local copies, waits for them, and re-layouts  108 us (16%)
  matrix products  83.5 us (13%)
  starting transfers between devices  60.9 us (9%)
  other arithmetic  36.2 us (5%)
  waiting for transfers between devices  28.2 us (4%)
    psum x2, blocking collectives, on_device(): group = lax.psum(local[:, None] * select[None, :], 'nodes')  257 us
    psum x1, blocking collectives, on_device(): lax.psum((jnp.sum(final * final), jnp.sum(right_side * right_side)), ('no...  78.1 us
    dot_general x4, matrix products, apply_op(): far = jnp.einsum('bkij,pbkj->pbi', off_mats, near, precision=hi)  43.3 us
    scatter-add x1, other arithmetic, on_device(): coarse_res = jax.ops.segment_sum(resid.T, agg_map, num_segments=NA_DEV).T  22.7 us
    dot_general x4, matrix products, apply_op(): own = jnp.einsum('bij,pbj->pbi', diag_mats, blocks, precision=hi)  21.2 us
    gather x3, local copies, waits for them, and re-layouts, on_device(): third = second + coarse_corr[:, agg_map]  19.7 us
    dot_general x3, matrix products, smooth(): jnp.einsum('bij,pbj->pbi', smooth_mats, field.reshape(terms, nblk, 64), p...  19 us
    ppermute x4, starting transfers between devices, extended_2(): lax.ppermute(lax.slice_in_dim(block, 0, width, axis=dim), axis, backward)  15.6 us
  transfers between devices with their start and end apart: 13, of which 3 were waited for; matrix products, arithmetic and copies ran while one was open for 20% of the time, Pallas kernels for 0%

commit v1 on v0

v1 whole, which is shorter than its diff:
```python
import functools

import jax
import jax.numpy as jnp
from jax import lax
from jax.experimental import pallas as pl
from jax.experimental.pallas import tpu as pltpu
from jax.sharding import PartitionSpec as P

NB = 64
H = 8
KB = 4
NA = 256
NOWN = 16
TERMS = 30
R = 32
R1 = R + NOWN
TILES = NB // 2
UN = 4
YC = 8
YS = 4
CS = 2
MESH = pl.DeviceIdType.MESH
F32 = jnp.float32
BF16 = jnp.bfloat16


def dot_nt(a, b, precision=None):
    return lax.dot_general(
        a, b, (((1,), (1,)), ((), ())), precision=precision, preferred_element_type=F32
    )


def dot_nn(a, b):
    return lax.dot_general(a, b, (((1,), (0,)), ((), ())), preferred_element_type=F32)


def split(v):
    hi = v.astype(BF16)
    return hi, (v - hi.astype(F32)).astype(BF16)


def swap(v):
    return pltpu.roll(v, 64, 1)


def kernel(
    zs,
    xs,
    col,
    send_list,
    rhs_hbm,
    diag_hbm,
    off_hbm,
    smooth_hbm,
    agg_hbm,
    owner_hbm,
    cdiag_hbm,
    cweight_hbm,
    cgain_hbm,
    out_hbm,
    ratio_ref,
    rhs_v,
    diag_v,
    off_v,
    smooth_v,
    agg_v,
    owner_v,
    cdiag_v,
    cweight_v,
    cgain_v,
    mats,
    fields,
    hot,
    b_f,
    x_f,
    r_f,
    w_f,
    c_x,
    c_r,
    tmp,
    sol_v,
    snd1,
    rcv1,
    snd2,
    rcv2,
    sum_a,
    sum_b,
    norm_a,
    norm_b,
    load_sem,
    halo_send,
    halo_recv,
    a_send,
    a_recv,
    b_send,
    b_recv,
    na_send,
    na_recv,
    nb_send,
    nb_recv,
):
    n = lax.axis_index("nodes")
    x = lax.axis_index("chaos")
    count = zs * YC
    z = n // YC
    yc = n % YC
    y = yc // CS
    c = yc % CS
    right = lax.rem(n + 1, count)
    left = lax.rem(n + count - 1, count)

    def node(zz, yy, cc):
        return (zz * YS + yy) * CS + cc

    loads = [
        pltpu.make_async_copy(src, dst, load_sem.at[i])
        for i, (src, dst) in enumerate(
            [
                (agg_hbm, agg_v),
                (owner_hbm, owner_v),
                (cdiag_hbm, cdiag_v),
                (cweight_hbm, cweight_v),
                (cgain_hbm, cgain_v),
                (smooth_hbm, smooth_v),
                (diag_hbm, diag_v),
                (rhs_hbm, rhs_v),
                (off_hbm, off_v),
            ]
        )
    ]
    for load in loads:
        load.start()

    peers_a = [(z * YC + lax.rem(yc + j, YC), x) for j in range(1, YC)]
    peers_b = [(lax.rem(z + j, zs) * YC + yc, x) for j in range(1, zs)]
    peers_na = [
        (node(z, lax.rem(y + j % YS, YS), c), lax.rem(x + j // YS, xs))
        for j in range(1, xs * YS)
    ]
    peers_nb = [
        (node(lax.rem(z + j // CS, zs), y, lax.rem(c + j % CS, CS)), x)
        for j in range(1, zs * CS)
    ]
    barrier = pltpu.get_barrier_semaphore()
    greeted = [(left, x), (right, x)] + peers_a + peers_b + peers_na + peers_nb
    for peer in greeted:
        pl.semaphore_signal(barrier, inc=1, device_id=peer, device_id_type=MESH)

    lane = lax.broadcasted_iota(jnp.int32, (1, 128), 1)
    low = lane < 64
    keep_low = low.astype(F32).astype(BF16)
    keep_high = (lane >= 64).astype(F32).astype(BF16)

    def pick(a, b):
        return jnp.where(low, a, b)

    def combine(out, rows):
        u = out[:rows]
        w = u + jnp.where(low, out[rows:], 0.0)
        return w + swap(w)

    def put(slot, blk, both, rows):
        hi, lo = split(both)
        fields[slot, blk, 0, 0:rows, :] = hi * keep_low
        fields[slot, blk, 0, rows : 2 * rows, :] = lo * keep_low
        fields[slot, blk, 1, 0:rows, :] = hi * keep_high
        fields[slot, blk, 1, rows : 2 * rows, :] = lo * keep_high

    def apply_a(slot, blk, rows):
        cols = [col[k, blk] for k in range(KB)]
        near = [
            fields[slot, cols[k], 0, 0 : 2 * rows, :] + fields[slot, cols[k + 1], 1, 0 : 2 * rows, :]
            for k in (0, 2)
        ]
        own = fields[slot, blk, 0, 0 : 2 * rows, :]
        lhs = jnp.concatenate(near + [own], axis=1)
        return combine(dot_nt(lhs, mats[blk]), rows)

    def apply_s(both, blk, rows):
        hi, lo = split(both)
        lhs = jnp.concatenate([hi * keep_high, lo * keep_high], axis=0)
        return combine(dot_nt(lhs, mats[blk, :, 256:384]), rows)

    def halo_copies(stage, snd, rcv, slot):
        return [
            pltpu.make_async_remote_copy(
                src_ref=snd.at[slot, side],
                dst_ref=rcv.at[slot, side],
                send_sem=halo_send.at[stage, side],
                recv_sem=halo_recv.at[stage, side],
                device_id=(left if side == 0 else right, x),
                device_id_type=MESH,
            )
            for side in (0, 1)
        ]

    def take_halo(copies, rcv, rslot, slot, rows):
        for side, base in ((1, NB), (0, NB + H)):
            copies[side].wait_recv()
            for m in range(H // 2):
                tile = rcv[rslot, side, m]
                other = swap(tile)
                put(slot, base + 2 * m, pick(tile, other), rows)
                put(slot, base + 2 * m + 1, pick(other, tile), rows)

    def export_from(ref, snd, slot):
        for side in (0, 1):
            for m in range(H // 2):
                first = send_list[side * H + 2 * m]
                second = send_list[side * H + 2 * m + 1]
                snd[slot, side, m] = pick(ref[first], ref[second])

    def loop(body, steps, unroll):
        def step(i, carry):
            body([i * unroll + j for j in range(unroll)])
            return carry

        lax.fori_loop(0, steps // unroll, step, 0)

    for load in loads[:5]:
        load.wait()
    inv = 1.0 / cdiag_v[...]
    gain = cgain_v[...] * inv
    weight = cweight_v[...]
    own_hot = (
        lax.broadcasted_iota(jnp.int32, (NOWN, NA), 0) == owner_v[...]
    ).astype(F32)
    rows_a = lax.broadcasted_iota(jnp.int32, (NA, 128), 0)

    def build_hot(ts):
        for t in ts:
            hot[t] = (rows_a == agg_v[pl.ds(t, 1), :]).astype(F32).astype(BF16)

    loop(build_hot, TILES, 2)

    g_hi, g_lo = split(own_hot * gain)
    g_lhs = jnp.concatenate([g_hi, g_lo], axis=0)

    def build_pg(ts):
        for t in ts:
            both = dot_nn(g_lhs, hot[t])
            tile = both[:NOWN] + both[NOWN:]
            other = swap(tile)
            x_f[2 * t, R:R1, :] = pick(tile, other)
            x_f[2 * t + 1, R:R1, :] = pick(other, tile)

    loop(build_pg, TILES, 4)

    def interleave(j, first, second):
        a, b = swap(first), swap(second)
        tmp[j, pl.ds(0, 32, stride=2), :] = pick(first, b)
        tmp[j, pl.ds(1, 32, stride=2), :] = pick(a, second)

    def settle(j, blk, at):
        hi, lo = split(tmp[j])
        mats[blk, 0:64, at : at + 128] = hi
        mats[blk, 64:128, at : at + 128] = lo

    def strided8(ref, blk):
        return ref[pl.ds((blk // 8) * 256 + blk % 8, 32, stride=8), :]

    for load in loads[5:8]:
        load.wait()

    def prep_own(bs):
        for j, blk in enumerate(bs):
            interleave(j, strided8(diag_v, blk), strided8(smooth_v, blk))
        for j, blk in enumerate(bs):
            settle(j, blk, 256)

    loop(prep_own, NB, UN)

    zero2 = jnp.zeros((2, 128), F32)

    def first_smooth(ts):
        for t in ts:
            tile = rhs_v[:, pl.ds(pl.multiple_of(t * 128, 128), 128)]
            tile = jnp.concatenate([tile, zero2], axis=0)
            other = swap(tile)
            for blk, both in ((2 * t, pick(tile, other)), (2 * t + 1, pick(other, tile))):
                b_f[blk] = both
                x_f[blk, 0:R, :] = apply_s(both, blk, R)
                put(0, blk, x_f[blk], R1)

    loop(first_smooth, TILES, 2)

    pl.semaphore_wait(barrier, len(greeted))
    export_from(x_f, snd1, 0)
    halo1 = halo_copies(0, snd1, rcv1, 0)
    for copy in halo1:
        copy.start()

    loads[8].wait()

    def prep_off(bs):
        for j, blk in enumerate(bs):
            parts = [off_v[pl.ds(blk * 128 + k, 32, stride=4), :] for k in range(KB)]
            interleave(2 * j, parts[0], parts[1])
            interleave(2 * j + 1, parts[2], parts[3])
        for j, blk in enumerate(bs):
            settle(2 * j, blk, 0)
            settle(2 * j + 1, blk, 128)

    loop(prep_off, NB, UN)

    none = jnp.zeros((NOWN, 128), F32)

    def second(blk):
        target = jnp.concatenate([b_f[blk], none], axis=0)
        resid = target - apply_a(0, blk, R1)
        return x_f[blk] + apply_s(resid, blk, R1)

    take_halo(halo1, rcv1, 0, 0, R1)

    def second_export(ms):
        done = [second(send_list[m]) for m in ms]
        for i in range(0, len(ms), 2):
            e_tile = pick(done[i], done[i + 1])
            snd1[1, ms[i] // H, (ms[i] % H) // 2] = e_tile

    loop(second_export, 2 * H, UN)
    halo2 = halo_copies(1, snd1, rcv1, 1)
    for copy in halo2:
        copy.start()

    def second_all(bs):
        done = [second(blk) for blk in bs]
        for blk, both in zip(bs, done):
            put(1, blk, both, R1)
            w_f[blk] = both

    loop(second_all, NB, UN)
    take_halo(halo2, rcv1, 1, 1, R1)

    def triple(tile):
        hi, lo = split(tile)
        return jnp.concatenate([hi, hi, lo], axis=0)

    def resid_all(bs):
        out = []
        for blk in bs:
            target = jnp.concatenate([b_f[blk], none], axis=0)
            out.append(target - apply_a(1, blk, R1))
        for i in range(0, len(bs), 2):
            t = bs[i] // 2
            tile = pick(out[i], out[i + 1])
            r_f[bs[i]] = out[i][:R]
            r_f[bs[i + 1]] = out[i + 1][:R]
            c_r[t] = triple(tile[R:])
            c_x[t] = triple(pick(w_f[bs[i], R:R1, :], w_f[bs[i + 1], R:R1, :]))

    loop(resid_all, NB, UN)

    def restrict(i, acc):
        for j in range(2):
            t = i * 2 + j
            hi, lo = split(pick(r_f[2 * t], r_f[2 * t + 1]))
            acc = acc + dot_nt(jnp.concatenate([hi, lo], axis=0), hot[t])
        return acc

    acc = lax.fori_loop(0, TILES // 2, restrict, jnp.zeros((2 * R, NA), F32))
    coarse = (acc[:R] + acc[R:]) * inv
    row = lax.broadcasted_iota(jnp.int32, (R, NA), 0)
    weighted = jnp.where(row == TERMS, gain, coarse) * weight
    part = dot_nt(own_hot, weighted, lax.Precision.HIGHEST)
    sum_a[0] = jnp.concatenate([part, jnp.zeros((NOWN, 128 - R), F32)], axis=1)
    copies_a = [
        pltpu.make_async_remote_copy(
            src_ref=sum_a.at[0],
            dst_ref=sum_a.at[j + 1],
            send_sem=a_send.at[j],
            recv_sem=a_recv.at[j],
            device_id=peer,
            device_id_type=MESH,
        )
        for j, peer in enumerate(peers_a)
    ]
    for copy in copies_a:
        copy.start()

    e_hi, e_lo = split(coarse)
    e_lhs = jnp.concatenate([e_hi, e_lo], axis=0)

    def prolong(ts):
        for t in ts:
            both = dot_nn(e_lhs, hot[t])
            tile = both[:R] + both[R:]
            other = swap(tile)
            for blk, dup in ((2 * t, pick(tile, other)), (2 * t + 1, pick(other, tile))):
                b_f[blk] = dup
                put(0, blk, dup, R)

    loop(prolong, TILES, 4)
    export_from(b_f, snd2, 0)
    halo3 = halo_copies(2, snd2, rcv2, 0)
    for copy in halo3:
        copy.start()
    for copy in copies_a:
        copy.wait_recv()
    sum_b[0] = jnp.sum(sum_a[...], axis=0)
    copies_b = [
        pltpu.make_async_remote_copy(
            src_ref=sum_b.at[0],
            dst_ref=sum_b.at[j + 1],
            send_sem=b_send.at[j],
            recv_sem=b_recv.at[j],
            device_id=peer,
            device_id_type=MESH,
        )
        for j, peer in enumerate(peers_b)
    ]
    for copy in copies_b:
        copy.start()
    take_halo(halo3, rcv2, 0, 0, R)

    def third(blk):
        resid = r_f[blk] - apply_a(0, blk, R)
        return resid, apply_s(resid, blk, R)

    def third_export(ms):
        done = [third(send_list[m])[1] for m in ms]
        for i in range(0, len(ms), 2):
            snd2[1, ms[i] // H, (ms[i] % H) // 2] = pick(done[i], done[i + 1])

    loop(third_export, 2 * H, UN)
    halo4 = halo_copies(3, snd2, rcv2, 1)
    for copy in halo4:
        copy.start()

    def third_all(bs):
        done = [third(blk) for blk in bs]
        for blk, (resid, step) in zip(bs, done):
            put(1, blk, step, R)
            x_f[blk, 0:R, :] = resid
            b_f[blk] = b_f[blk] + step + w_f[blk, 0:R, :]

    loop(third_all, NB, UN)

    for copy in copies_b:
        copy.wait_recv()
    total = jnp.sum(sum_b[...], axis=0)[:, 0:R]
    total = total * (1.0 + total[:, TERMS : TERMS + 1])
    keep = lax.broadcasted_iota(jnp.int32, (NOWN, R), 1) < TERMS
    s_hi, s_lo = split(jnp.where(keep, total, 0.0).T)
    s_lhs = jnp.concatenate([s_hi, s_lo, s_hi], axis=1)

    def finish(ts):
        for t in ts:
            tile = pick(b_f[2 * t], b_f[2 * t + 1]) + dot_nn(s_lhs, c_x[t])
            sol_v[:, pl.ds(pl.multiple_of(t * 128, 128), 128)] = tile[:TERMS]

    loop(finish, TILES, 4)
    store = pltpu.make_async_copy(sol_v, out_hbm, load_sem.at[0])
    store.start()

    take_halo(halo4, rcv2, 1, 1, R)

    def final(i, acc):
        for j in range(2):
            t = i * 2 + j
            parts = [x_f[blk, 0:R, :] - apply_a(1, blk, R) for blk in (2 * t, 2 * t + 1)]
            tile = pick(parts[0], parts[1]) + dot_nn(s_lhs, c_r[t])
            acc = acc + tile * tile
        return acc

    acc = lax.fori_loop(0, TILES // 2, final, jnp.zeros((R, 128), F32))

    def right_norm(i, acc):
        tile = rhs_v[:, pl.ds(pl.multiple_of(i * 128, 128), 128)]
        return acc + tile * tile

    acc_b = lax.fori_loop(0, TILES, right_norm, jnp.zeros((TERMS, 128), F32))
    line = lax.broadcasted_iota(jnp.int32, (8, 128), 0)
    norm_a[0] = jnp.where(
        line == 0,
        jnp.sum(acc, axis=0, keepdims=True),
        jnp.where(line == 1, jnp.sum(acc_b, axis=0, keepdims=True), 0.0),
    )
    copies_na = [
        pltpu.make_async_remote_copy(
            src_ref=norm_a.at[0],
            dst_ref=norm_a.at[j + 1],
            send_sem=na_send.at[j],
            recv_sem=na_recv.at[j],
            device_id=peer,
            device_id_type=MESH,
        )
        for j, peer in enumerate(peers_na)
    ]
    for copy in copies_na:
        copy.start()
    for copy in copies_na:
        copy.wait_recv()
    norm_b[0] = jnp.sum(norm_a[...], axis=0)
    copies_nb = [
        pltpu.make_async_remote_copy(
            src_ref=norm_b.at[0],
            dst_ref=norm_b.at[j + 1],
            send_sem=nb_send.at[j],
            recv_sem=nb_recv.at[j],
            device_id=peer,
            device_id_type=MESH,
        )
        for j, peer in enumerate(peers_nb)
    ]
    for copy in copies_nb:
        copy.start()
    for copy in copies_nb:
        copy.wait_recv()
    sums = jnp.sum(jnp.sum(norm_b[...], axis=0), axis=1, keepdims=True)
    ratio_ref[...] = jnp.sqrt(sums[0:1] / (sums[1:2] + 1e-6))

    for copies in (halo1, halo2, halo3, halo4, copies_a, copies_b, copies_na, copies_nb):
        for copy in copies:
            copy.wait_send()
    store.wait()


def on_device(
    zs,
    xs,
    right_side,
    diag_blocks,
    off_blocks,
    smoother,
    col_index,
    send_list,
    agg_map,
    owner_map,
    coarse_diag,
    coarse_weight,
    coarse_gain,
):
    def rows_of(v):
        return v.reshape(8, 8, 32, 128).transpose(0, 2, 1, 3).reshape(NB * 32, 128)

    off = off_blocks.reshape(NB, KB, 32, 128).transpose(0, 2, 1, 3).reshape(NB * KB * 32, 128)
    hbm = pl.BlockSpec(memory_space=pl.ANY)
    smem = pl.BlockSpec(memory_space=pltpu.SMEM)
    dma = pltpu.SemaphoreType.DMA
    scratch = [
        pltpu.VMEM((TERMS, NB * 64), F32),
        pltpu.VMEM((NB * 32, 128), F32),
        pltpu.VMEM((NB * KB * 32, 128), F32),
        pltpu.VMEM((NB * 32, 128), F32),
        pltpu.VMEM((TILES, 128), jnp.int32),
        pltpu.VMEM((1, NA), jnp.int32),
        pltpu.VMEM((1, NA), F32),
        pltpu.VMEM((1, NA), F32),
        pltpu.VMEM((1, NA), F32),
        pltpu.VMEM((NB, 128, 384), BF16),
        pltpu.VMEM((2, NB + 2 * H, 2, 2 * R1, 128), BF16),
        pltpu.VMEM((TILES, NA, 128), BF16),
        pltpu.VMEM((NB, R, 128), F32),
        pltpu.VMEM((NB, R1, 128), F32),
        pltpu.VMEM((NB, R, 128), F32),
        pltpu.VMEM((NB, R1, 128), F32),
        pltpu.VMEM((TILES, 3 * NOWN, 128), BF16),
        pltpu.VMEM((TILES, 3 * NOWN, 128), BF16),
        pltpu.VMEM((2 * UN, 64, 128), F32),
        pltpu.VMEM((TERMS, NB * 64), F32),
        pltpu.VMEM((2, 2, H // 2, R1, 128), F32),
        pltpu.VMEM((2, 2, H // 2, R1, 128), F32),
        pltpu.VMEM((2, 2, H // 2, R, 128), F32),
        pltpu.VMEM((2, 2, H // 2, R, 128), F32),
        pltpu.VMEM((YC, NOWN, 128), F32),
        pltpu.VMEM((zs, NOWN, 128), F32),
        pltpu.VMEM((xs * YS, 8, 128), F32),
        pltpu.VMEM((zs * CS, 8, 128), F32),
        dma((9,)),
        dma((4, 2)),
        dma((4, 2)),
        dma((YC,)),
        dma((YC,)),
        dma((zs,)),
        dma((zs,)),
        dma((xs * YS,)),
        dma((xs * YS,)),
        dma((zs * CS,)),
        dma((zs * CS,)),
    ]
    out, ratio = pl.pallas_call(
        functools.partial(kernel, zs, xs),
        out_shape=(
            jax.ShapeDtypeStruct((TERMS, NB * 64), F32),
            jax.ShapeDtypeStruct((1, 1), F32),
        ),
        in_specs=[smem, smem] + [hbm] * 9,
        out_specs=(hbm, pl.BlockSpec(memory_space=pltpu.VMEM)),
        scratch_shapes=scratch,
        compiler_params=pltpu.CompilerParams(
            collective_id=0, has_side_effects=True, vmem_limit_bytes=56 * 1024 * 1024
        ),
    )(
        col_index.T,
        send_list,
        right_side,
        rows_of(diag_blocks),
        off,
        rows_of(smoother),
        agg_map.reshape(TILES, 128),
        owner_map.reshape(1, NA),
        coarse_diag.reshape(1, NA),
        coarse_weight.reshape(1, NA),
        coarse_gain.reshape(1, NA),
    )
    return out, ratio.reshape(())


def solution(mesh):
    placed = (
        P("chaos", "nodes"),
        P("nodes", None),
        P("nodes", None, None),
        P("nodes", None),
        P("nodes", None),
        P("nodes"),
        P("nodes"),
        P("nodes", None),
        P("nodes"),
        P("nodes"),
        P("nodes"),
    )
    return jax.shard_map(
        functools.partial(on_device, mesh.shape["nodes"] // YC, mesh.shape["chaos"]),
        mesh=mesh,
        in_specs=placed,
        out_specs=(P("chaos", "nodes"), P()),
        check_vma=False,
    )
```

time: 659 us -> 108 us (0.16)
  blocking collectives: 335 us -> 0 us
  local copies, waits for them, and re-layouts: 108 us -> 1.87 us
  Pallas kernels: 0 us -> 103 us
  matrix products: 83.5 us -> 0 us
  starting transfers between devices: 60.9 us -> 0 us
  other arithmetic: 36.2 us -> 0 us
  waiting for transfers between devices: 28.2 us -> 0 us
    psum x3 -> x0, blocking collectives: 335 us -> none  [the longest x2 257 us: on_device(): group = lax.psum(local[:, None] * select[None, :], 'nodes')]
    pallas_call x0 -> x1, Pallas kernels: none -> 103 us  [on_device(): pl.pallas_call(functools.partial(kernel, zs, xs), out_shape=(jax.ShapeDty...]
    dot_general x11 -> x0, matrix products: 83.5 us -> none  [the longest x4 43.3 us: apply_op(): far = jnp.einsum('bkij,pbkj->pbi', off_mats, near, precision=hi)]
    reshape x27 -> x0, local copies, waits for them, and re-layouts: 43.9 us -> none  [the longest x8 12.6 us: apply_op(): jnp.concatenate([field, padded[:, :rim], padded[:, 3 * rim:]], 1)]
    gather x16 -> x0, local copies, waits for them, and re-layouts: 39.7 us -> none  [the longest x3 19.7 us: on_device(): third = second + coarse_corr[:, agg_map]]
    all_to_all x5 -> x0, starting transfers between devices: 38.6 us -> none  [the longest x1 12.7 us: on_device(): lax.all_to_all(packed_diag, 'nodes', split_axis=0, concat_axis=0, tiled=T...]
    all_to_all x5 -> x0, waiting for transfers between devices: 28.2 us -> none  [the longest x1 10.1 us: on_device(): lax.all_to_all(packed_res, 'nodes', split_axis=0, concat_axis=0, tiled=True)]
    scatter-add x1 -> x0, other arithmetic: 22.7 us -> none  [on_device(): coarse_res = jax.ops.segment_sum(resid.T, agg_map, num_segments=NA_DEV).T]
  transfers between devices with their start and end apart: 13 -> 0, of which waited for: 3 -> 0; matrix products, arithmetic and copies ran while one was open for 20% -> 0% of each run, Pallas kernels for 0% -> 0%
where the time goes in v1:
time: 108 us; the launch traced here: 107 us
  Pallas kernels  103 us (95%)
  between operations  2.34 us (2%)
  local copies, waits for them, and re-layouts  1.87 us (2%)
    pallas_call x1, Pallas kernels, on_device(): pl.pallas_call(functools.partial(kernel, zs, xs), out_shape=(jax.ShapeDty...  103 us

profile of v1, /device:TPU:1, one launch (start us, length us, event | category | flops | bytes accessed | tf_op | source)
XLA Modules:
  0.0 107.3 jit_solution(3611147491190015445)
XLA Ops:
  0.6 103.1 %shard_map.122 = (f32[30,4096]{1,0:T(8,128)}, f32[1,1]{1,0:T(1,128)}) custom-call(s32[4,64]{1,0:T(4,128)} %bitcast.26, s32[16]{0:T(128)} %send_list.1, f32[30,4096]{1,0:T(8,128)} %rhs_hbm.1, f32[2048,128]{1,0:T(8,128)} %bitcast.23, f32[8192,128]{1,0:T(8,128)} %bitcast.22, f32[2048,128]{1,0:T(8,128)} %bitcast.24, s32[32,128]{1,0:T(8,128)} %bitcast.25, ...), custom_call_target="tpu_custom_call" | custom-call | tf_op jit(solution)/shard_map/pallas_call | solution.py:583
  103.8 1.9 %copy.16 = f32[30,4096]{1,0:T(8,128)} copy(f32[30,4096]{1,0:T(8,128)} %get-tuple-element.8) | data formatting | bytes 983040

commit v2 on v1

--- a/solution.py
+++ b/solution.py
@@ -1,4 +1,5 @@
 import functools
+import itertools
 
 import jax
 import jax.numpy as jnp
@@ -16,7 +17,7 @@
 R = 32
 R1 = R + NOWN
 TILES = NB // 2
-UN = 4
+UN = 32
 YC = 8
 YS = 4
 CS = 2
@@ -86,8 +87,7 @@
     rcv2,
     sum_a,
     sum_b,
-    norm_a,
-    norm_b,
+    norm_v,
     load_sem,
     halo_send,
     halo_recv,
@@ -95,10 +95,8 @@
     a_recv,
     b_send,
     b_recv,
-    na_send,
-    na_recv,
-    nb_send,
-    nb_recv,
+    n_send,
+    n_recv,
 ):
     n = lax.axis_index("nodes")
     x = lax.axis_index("chaos")
@@ -134,16 +132,23 @@
 
     peers_a = [(z * YC + lax.rem(yc + j, YC), x) for j in range(1, YC)]
     peers_b = [(lax.rem(z + j, zs) * YC + yc, x) for j in range(1, zs)]
-    peers_na = [
-        (node(z, lax.rem(y + j % YS, YS), c), lax.rem(x + j // YS, xs))
-        for j in range(1, xs * YS)
-    ]
-    peers_nb = [
-        (node(lax.rem(z + j // CS, zs), y, lax.rem(c + j % CS, CS)), x)
-        for j in range(1, zs * CS)
-    ]
+    dims = {"z": zs, "y": YS, "c": CS, "x": xs}
+    at = {"z": z, "y": y, "c": c, "x": x}
+
+    def group(axes):
+        peers = []
+        for offs in itertools.product(*[range(dims[a]) for a in axes]):
+            if any(offs):
+                to = dict(at)
+                for a, o in zip(axes, offs):
+                    if o:
+                        to[a] = lax.rem(at[a] + o, dims[a])
+                peers.append((node(to["z"], to["y"], to["c"]), to["x"]))
+        return peers
+
+    norm_groups = [group(axes) for axes in ['xy', 'zc']]
     barrier = pltpu.get_barrier_semaphore()
-    greeted = [(left, x), (right, x)] + peers_a + peers_b + peers_na + peers_nb
+    greeted = [(left, x), (right, x)] + peers_a + peers_b + sum(norm_groups, [])
     for peer in greeted:
         pl.semaphore_signal(barrier, inc=1, device_id=peer, device_id_type=MESH)
 
@@ -175,12 +180,12 @@
         ]
         own = fields[slot, blk, 0, 0 : 2 * rows, :]
         lhs = jnp.concatenate(near + [own], axis=1)
-        return combine(dot_nt(lhs, mats[blk]), rows)
+        return combine(dot_nn(lhs, mats[blk]), rows)
 
     def apply_s(both, blk, rows):
         hi, lo = split(both)
         lhs = jnp.concatenate([hi * keep_high, lo * keep_high], axis=0)
-        return combine(dot_nt(lhs, mats[blk, :, 256:384]), rows)
+        return combine(dot_nn(lhs, mats[blk, 256:384, :]), rows)
 
     def halo_copies(stage, snd, rcv, slot):
         return [
@@ -232,7 +237,7 @@
         for t in ts:
             hot[t] = (rows_a == agg_v[pl.ds(t, 1), :]).astype(F32).astype(BF16)
 
-    loop(build_hot, TILES, 2)
+    loop(build_hot, TILES, 4)
 
     g_hi, g_lo = split(own_hot * gain)
     g_lhs = jnp.concatenate([g_hi, g_lo], axis=0)
@@ -245,7 +250,7 @@
             x_f[2 * t, R:R1, :] = pick(tile, other)
             x_f[2 * t + 1, R:R1, :] = pick(other, tile)
 
-    loop(build_pg, TILES, 4)
+    loop(build_pg, TILES, 8)
 
     def interleave(j, first, second):
         a, b = swap(first), swap(second)
@@ -254,8 +259,7 @@
 
     def settle(j, blk, at):
         hi, lo = split(tmp[j])
-        mats[blk, 0:64, at : at + 128] = hi
-        mats[blk, 64:128, at : at + 128] = lo
+        mats[blk, at : at + 128, :] = jnp.concatenate([hi, lo], axis=0).T
 
     def strided8(ref, blk):
         return ref[pl.ds((blk // 8) * 256 + blk % 8, 32, stride=8), :]
@@ -283,7 +287,7 @@
                 x_f[blk, 0:R, :] = apply_s(both, blk, R)
                 put(0, blk, x_f[blk], R1)
 
-    loop(first_smooth, TILES, 2)
+    loop(first_smooth, TILES, 16)
 
     pl.semaphore_wait(barrier, len(greeted))
     export_from(x_f, snd1, 0)
@@ -313,24 +317,28 @@
 
     take_halo(halo1, rcv1, 0, 0, R1)
 
-    def second_export(ms):
-        done = [second(send_list[m]) for m in ms]
-        for i in range(0, len(ms), 2):
-            e_tile = pick(done[i], done[i + 1])
-            snd1[1, ms[i] // H, (ms[i] % H) // 2] = e_tile
-
-    loop(second_export, 2 * H, UN)
+    def second_a(bs):
+        out = []
+        for blk in bs:
+            target = jnp.concatenate([b_f[blk], none], axis=0)
+            out.append(target - apply_a(0, blk, R1))
+        for blk, r in zip(bs, out):
+            w_f[blk] = r
+
+    loop(second_a, NB, UN)
+
+    def second_all(bs):
+        done = [x_f[blk] + apply_s(w_f[blk], blk, R1) for blk in bs]
+        for blk, both in zip(bs, done):
+            put(1, blk, both, R1)
+            w_f[blk] = both
+
+    loop(second_all, NB, UN)
+    export_from(w_f, snd1, 1)
     halo2 = halo_copies(1, snd1, rcv1, 1)
     for copy in halo2:
         copy.start()
 
-    def second_all(bs):
-        done = [second(blk) for blk in bs]
-        for blk, both in zip(bs, done):
-            put(1, blk, both, R1)
-            w_f[blk] = both
-
-    loop(second_all, NB, UN)
     take_halo(halo2, rcv1, 1, 1, R1)
 
     def triple(tile):
@@ -353,13 +361,13 @@
     loop(resid_all, NB, UN)
 
     def restrict(i, acc):
-        for j in range(2):
-            t = i * 2 + j
+        for j in range(16):
+            t = i * 16 + j
             hi, lo = split(pick(r_f[2 * t], r_f[2 * t + 1]))
             acc = acc + dot_nt(jnp.concatenate([hi, lo], axis=0), hot[t])
         return acc
 
-    acc = lax.fori_loop(0, TILES // 2, restrict, jnp.zeros((2 * R, NA), F32))
+    acc = lax.fori_loop(0, TILES // 16, restrict, jnp.zeros((2 * R, NA), F32))
     coarse = (acc[:R] + acc[R:]) * inv
     row = lax.broadcasted_iota(jnp.int32, (R, NA), 0)
     weighted = jnp.where(row == TERMS, gain, coarse) * weight
@@ -391,7 +399,7 @@
                 b_f[blk] = dup
                 put(0, blk, dup, R)
 
-    loop(prolong, TILES, 4)
+    loop(prolong, TILES, 8)
     export_from(b_f, snd2, 0)
     halo3 = halo_copies(2, snd2, rcv2, 0)
     for copy in halo3:
@@ -418,24 +426,24 @@
         resid = r_f[blk] - apply_a(0, blk, R)
         return resid, apply_s(resid, blk, R)
 
-    def third_export(ms):
-        done = [third(send_list[m])[1] for m in ms]
-        for i in range(0, len(ms), 2):
-            snd2[1, ms[i] // H, (ms[i] % H) // 2] = pick(done[i], done[i + 1])
-
-    loop(third_export, 2 * H, UN)
+    def third_a(bs):
+        out = [r_f[blk] - apply_a(0, blk, R) for blk in bs]
+        for blk, r in zip(bs, out):
+            x_f[blk, 0:R, :] = r
+
+    loop(third_a, NB, UN)
+
+    def third_all(bs):
+        done = [apply_s(x_f[blk, 0:R, :], blk, R) for blk in bs]
+        for blk, step in zip(bs, done):
+            put(1, blk, step, R)
+            r_f[blk] = step
+
+    loop(third_all, NB, UN)
+    export_from(r_f, snd2, 1)
     halo4 = halo_copies(3, snd2, rcv2, 1)
     for copy in halo4:
         copy.start()
-
-    def third_all(bs):
-        done = [third(blk) for blk in bs]
-        for blk, (resid, step) in zip(bs, done):
-            put(1, blk, step, R)
-            x_f[blk, 0:R, :] = resid
-            b_f[blk] = b_f[blk] + step + w_f[blk, 0:R, :]
-
-    loop(third_all, NB, UN)
 
     for copy in copies_b:
         copy.wait_recv()
@@ -447,24 +455,25 @@
 
     def finish(ts):
         for t in ts:
-            tile = pick(b_f[2 * t], b_f[2 * t + 1]) + dot_nn(s_lhs, c_x[t])
+            parts = [b_f[blk] + r_f[blk] + w_f[blk, 0:R, :] for blk in (2 * t, 2 * t + 1)]
+            tile = pick(parts[0], parts[1]) + dot_nn(s_lhs, c_x[t])
             sol_v[:, pl.ds(pl.multiple_of(t * 128, 128), 128)] = tile[:TERMS]
 
-    loop(finish, TILES, 4)
+    loop(finish, TILES, 8)
     store = pltpu.make_async_copy(sol_v, out_hbm, load_sem.at[0])
     store.start()
 
     take_halo(halo4, rcv2, 1, 1, R)
 
     def final(i, acc):
-        for j in range(2):
-            t = i * 2 + j
+        for j in range(16):
+            t = i * 16 + j
             parts = [x_f[blk, 0:R, :] - apply_a(1, blk, R) for blk in (2 * t, 2 * t + 1)]
             tile = pick(parts[0], parts[1]) + dot_nn(s_lhs, c_r[t])
             acc = acc + tile * tile
         return acc
 
-    acc = lax.fori_loop(0, TILES // 2, final, jnp.zeros((R, 128), F32))
+    acc = lax.fori_loop(0, TILES // 16, final, jnp.zeros((R, 128), F32))
 
     def right_norm(i, acc):
         tile = rhs_v[:, pl.ds(pl.multiple_of(i * 128, 128), 128)]
@@ -472,46 +481,41 @@
 
     acc_b = lax.fori_loop(0, TILES, right_norm, jnp.zeros((TERMS, 128), F32))
     line = lax.broadcasted_iota(jnp.int32, (8, 128), 0)
-    norm_a[0] = jnp.where(
+    norm_v[0, 0] = jnp.where(
         line == 0,
         jnp.sum(acc, axis=0, keepdims=True),
         jnp.where(line == 1, jnp.sum(acc_b, axis=0, keepdims=True), 0.0),
     )
-    copies_na = [
-        pltpu.make_async_remote_copy(
-            src_ref=norm_a.at[0],
-            dst_ref=norm_a.at[j + 1],
-            send_sem=na_send.at[j],
-            recv_sem=na_recv.at[j],
-            device_id=peer,
-            device_id_type=MESH,
-        )
-        for j, peer in enumerate(peers_na)
-    ]
-    for copy in copies_na:
-        copy.start()
-    for copy in copies_na:
-        copy.wait_recv()
-    norm_b[0] = jnp.sum(norm_a[...], axis=0)
-    copies_nb = [
-        pltpu.make_async_remote_copy(
-            src_ref=norm_b.at[0],
-            dst_ref=norm_b.at[j + 1],
-            send_sem=nb_send.at[j],
-            recv_sem=nb_recv.at[j],
-            device_id=peer,
-            device_id_type=MESH,
-        )
-        for j, peer in enumerate(peers_nb)
-    ]
-    for copy in copies_nb:
-        copy.start()
-    for copy in copies_nb:
-        copy.wait_recv()
-    sums = jnp.sum(jnp.sum(norm_b[...], axis=0), axis=1, keepdims=True)
+    norm_copies = []
+    for g, peers in enumerate(norm_groups):
+        if g:
+            norm_v[g, 0] = jnp.sum(norm_v[g - 1, 0 : len(norm_groups[g - 1]) + 1], axis=0)
+        if not peers:
+            continue
+        copies = [
+            pltpu.make_async_remote_copy(
+                src_ref=norm_v.at[g, 0],
+                dst_ref=norm_v.at[g, j + 1],
+                send_sem=n_send.at[g],
+                recv_sem=n_recv.at[g],
+                device_id=peer,
+                device_id_type=MESH,
+            )
+            for j, peer in enumerate(peers)
+        ]
+        for copy in copies:
+            copy.start()
+        landed = norm_v.at[g, 1 : len(peers) + 1]
+        pltpu.make_async_copy(landed, landed, n_recv.at[g]).wait()
+        norm_copies.append((g, landed))
+    last = len(norm_groups) - 1
+    sums = jnp.sum(norm_v[last, 0 : len(norm_groups[last]) + 1], axis=0)
+    sums = jnp.sum(sums, axis=1, keepdims=True)
     ratio_ref[...] = jnp.sqrt(sums[0:1] / (sums[1:2] + 1e-6))
-
-    for copies in (halo1, halo2, halo3, halo4, copies_a, copies_b, copies_na, copies_nb):
+    for g, landed in norm_copies:
+        pltpu.make_async_copy(landed, landed, n_send.at[g]).wait()
+
+    for copies in (halo1, halo2, halo3, halo4, copies_a, copies_b):
         for copy in copies:
             copy.wait_send()
     store.wait()
@@ -549,7 +553,7 @@
         pltpu.VMEM((1, NA), F32),
         pltpu.VMEM((1, NA), F32),
         pltpu.VMEM((1, NA), F32),
-        pltpu.VMEM((NB, 128, 384), BF16),
+        pltpu.VMEM((NB, 384, 128), BF16),
         pltpu.VMEM((2, NB + 2 * H, 2, 2 * R1, 128), BF16),
         pltpu.VMEM((TILES, NA, 128), BF16),
         pltpu.VMEM((NB, R, 128), F32),
@@ -566,8 +570,7 @@
         pltpu.VMEM((2, 2, H // 2, R, 128), F32),
         pltpu.VMEM((YC, NOWN, 128), F32),
         pltpu.VMEM((zs, NOWN, 128), F32),
-        pltpu.VMEM((xs * YS, 8, 128), F32),
-        pltpu.VMEM((zs * CS, 8, 128), F32),
+        pltpu.VMEM((2, 64, 8, 128), F32),
         dma((9,)),
         dma((4, 2)),
         dma((4, 2)),
@@ -575,10 +578,8 @@
         dma((YC,)),
         dma((zs,)),
         dma((zs,)),
-        dma((xs * YS,)),
-        dma((xs * YS,)),
-        dma((zs * CS,)),
-        dma((zs * CS,)),
+        dma((2,)),
+        dma((2,)),
     ]
     out, ratio = pl.pallas_call(
         functools.partial(kernel, zs, xs),

time: 108 us -> 58.2 us (0.54)
  Pallas kernels: 103 us -> 53.8 us
    pallas_call x1, Pallas kernels: 103 us -> 53.8 us  [on_device(): pl.pallas_call(functools.partial(kernel, zs, xs), out_shape=(jax.ShapeDty...]
where the time goes in v2:
time: 58.2 us; the launch traced here: 58 us
  Pallas kernels  53.8 us (92%)
  between operations  2.34 us (4%)
  local copies, waits for them, and re-layouts  1.87 us (3%)
    pallas_call x1, Pallas kernels, on_device(): pl.pallas_call(functools.partial(kernel, zs, xs), out_shape=(jax.ShapeDty...  53.8 us
    unnamed x1, local copies, waits for them, and re-layouts  1.87 us

profile of v2, /device:TPU:1, one launch (start us, length us, event | category | flops | bytes accessed | tf_op | source)
XLA Modules:
  0.0 58.0 jit_solution(9343637531305243715)
XLA Ops:
  0.6 53.8 %shard_map.122 = (f32[30,4096]{1,0:T(8,128)}, f32[1,1]{1,0:T(1,128)}) custom-call(s32[4,64]{1,0:T(4,128)} %bitcast.26, s32[16]{0:T(128)} %send_list.1, f32[30,4096]{1,0:T(8,128)} %rhs_hbm.1, f32[2048,128]{1,0:T(8,128)} %bitcast.23, f32[8192,128]{1,0:T(8,128)} %bitcast.22, f32[2048,128]{1,0:T(8,128)} %bitcast.24, s32[32,128]{1,0:T(8,128)} %bitcast.25, ...), custom_call_target="tpu_custom_call" | custom-call | tf_op jit(solution)/shard_map/pallas_call | solution.py:584
  54.4 1.9 %copy.16 = f32[30,4096]{1,0:T(8,128)} copy(f32[30,4096]{1,0:T(8,128)} %get-tuple-element.8) | data formatting | bytes 983040

commit v3 on v2

v3 whole, which is shorter than its diff:
```python
import functools
import itertools

import jax
import jax.numpy as jnp
from jax import lax
from jax.experimental import pallas as pl
from jax.experimental.pallas import tpu as pltpu
from jax.sharding import PartitionSpec as P

NB = 64
H = 8
KB = 4
NA = 256
NOWN = 16
TERMS = 30
R = 32
TILES = NB // 2
PAIRS = NB // 4
UN = 32
YC = 8
YS = 4
CS = 2
MESH = pl.DeviceIdType.MESH
F32 = jnp.float32
BF16 = jnp.bfloat16


def dot_nt(a, b, precision=None):
    return lax.dot_general(
        a, b, (((1,), (1,)), ((), ())), precision=precision, preferred_element_type=F32
    )


def dot_nn(a, b):
    return lax.dot_general(a, b, (((1,), (0,)), ((), ())), preferred_element_type=F32)


def split(v):
    hi = v.astype(BF16)
    return hi, (v - hi.astype(F32)).astype(BF16)


def swap(v):
    return pltpu.roll(v, 64, 1)


def kernel(
    zs,
    xs,
    col,
    send_list,
    rhs_hbm,
    diag_hbm,
    off_hbm,
    smooth_hbm,
    agg_hbm,
    owner_hbm,
    cdiag_hbm,
    cweight_hbm,
    cgain_hbm,
    out_hbm,
    ratio_ref,
    rhs_v,
    diag_v,
    off_v,
    smooth_v,
    agg_v,
    owner_v,
    cdiag_v,
    cweight_v,
    cgain_v,
    mats,
    fields,
    owner_fields,
    hot,
    hot_t,
    b_f,
    e_f,
    g_f,
    x_f,
    r_f,
    w_f,
    c_x,
    c_r,
    tmp,
    sol_v,
    snd,
    rcv,
    snd_e,
    rcv_e,
    sum_a,
    sum_b,
    norm_v,
    load_sem,
    halo_send,
    halo_recv,
    a_send,
    a_recv,
    b_send,
    b_recv,
    n_send,
    n_recv,
):
    n = lax.axis_index("nodes")
    x = lax.axis_index("chaos")
    count = zs * YC
    z = n // YC
    yc = n % YC
    y = yc // CS
    c = yc % CS
    right = lax.rem(n + 1, count)
    left = lax.rem(n + count - 1, count)

    def node(zz, yy, cc):
        return (zz * YS + yy) * CS + cc

    loads = [
        pltpu.make_async_copy(src, dst, load_sem.at[i])
        for i, (src, dst) in enumerate(
            [
                (agg_hbm, agg_v),
                (owner_hbm, owner_v),
                (cdiag_hbm, cdiag_v),
                (cweight_hbm, cweight_v),
                (cgain_hbm, cgain_v),
                (smooth_hbm, smooth_v),
                (diag_hbm, diag_v),
                (rhs_hbm, rhs_v),
                (off_hbm, off_v),
            ]
        )
    ]
    for load in loads:
        load.start()

    dims = {"z": zs, "y": YS, "c": CS, "x": xs}
    at = {"z": z, "y": y, "c": c, "x": x}

    def group(axes):
        steps = [offs for offs in itertools.product(*[range(dims[a]) for a in axes]) if any(offs)]
        steps.sort(key=lambda offs: -sum(min(o, dims[a] - o) for a, o in zip(axes, offs)))
        peers = []
        for offs in steps:
            to = dict(at)
            for a, o in zip(axes, offs):
                if o:
                    to[a] = lax.rem(at[a] + o, dims[a])
            peers.append((node(to["z"], to["y"], to["c"]), to["x"]))
        return peers

    peers_a = group("yc")
    peers_b = group("z")

    norm_groups = [group(axes) for axes in ['xy', 'zc']]
    barrier = pltpu.get_barrier_semaphore()
    greeted = [(left, x), (right, x)] + peers_a + peers_b + sum(norm_groups, [])
    for peer in greeted:
        pl.semaphore_signal(barrier, inc=1, device_id=peer, device_id_type=MESH)

    lane = lax.broadcasted_iota(jnp.int32, (1, 128), 1)
    low = lane < 64
    keep_low = low.astype(F32).astype(BF16)
    keep_high = (lane >= 64).astype(F32).astype(BF16)

    def pick(a, b):
        return jnp.where(low, a, b)

    def combine(out, rows):
        u = out[:rows]
        w = u + jnp.where(low, out[rows:], 0.0)
        return w + swap(w)

    def put(store, slot, blk, both, rows):
        hi, lo = split(both)
        store[slot, blk, 0, 0:rows, :] = hi * keep_low
        store[slot, blk, 0, rows : 2 * rows, :] = lo * keep_low
        store[slot, blk, 1, 0:rows, :] = hi * keep_high
        store[slot, blk, 1, rows : 2 * rows, :] = lo * keep_high

    def apply_a(store, slot, blk, rows):
        cols = [col[k, blk] for k in range(KB)]
        near = [
            store[slot, cols[k], 0, 0 : 2 * rows, :] + store[slot, cols[k + 1], 1, 0 : 2 * rows, :]
            for k in (0, 2)
        ]
        own = store[slot, blk, 0, 0 : 2 * rows, :]
        lhs = jnp.concatenate(near + [own], axis=1)
        return combine(dot_nn(lhs, mats[blk]), rows)

    def apply_s(both, blk, rows):
        hi, lo = split(both)
        lhs = jnp.concatenate([hi * keep_high, lo * keep_high], axis=0)
        return combine(dot_nn(lhs, mats[blk, 256:384, :]), rows)

    def halo_copies(stage, src, dst, slot):
        return [
            pltpu.make_async_remote_copy(
                src_ref=src.at[slot, side],
                dst_ref=dst.at[slot, side],
                send_sem=halo_send.at[stage, side],
                recv_sem=halo_recv.at[stage, side],
                device_id=(left if side == 0 else right, x),
                device_id_type=MESH,
            )
            for side in (0, 1)
        ]

    def send_halo(stage, ref, src, dst, slot):
        export_from(ref, src, slot)
        copies = halo_copies(stage, src, dst, slot)
        for copy in copies:
            copy.start()
        return copies

    def take_halo(copies, store, slot, src, rslot, rows):
        for side, base in ((1, NB), (0, NB + H)):
            copies[side].wait_recv()
            for m in range(H // 2):
                tile = src[rslot, side, m]
                other = swap(tile)
                put(store, slot, base + 2 * m, pick(tile, other), rows)
                put(store, slot, base + 2 * m + 1, pick(other, tile), rows)

    def export_from(ref, dst, slot):
        for side in (0, 1):
            for m in range(H // 2):
                first = send_list[side * H + 2 * m]
                second = send_list[side * H + 2 * m + 1]
                dst[slot, side, m] = pick(ref[first], ref[second])

    def loop(body, steps, unroll):
        def step(i, carry):
            body([i * unroll + j for j in range(unroll)])
            return carry

        lax.fori_loop(0, steps // unroll, step, 0)

    def interleave(j, first, second):
        a, b = swap(first), swap(second)
        tmp[j, pl.ds(0, 32, stride=2), :] = pick(first, b)
        tmp[j, pl.ds(1, 32, stride=2), :] = pick(a, second)

    def settle(j, blk, at):
        hi, lo = split(tmp[j])
        mats[blk, at : at + 128, :] = jnp.concatenate([hi, lo], axis=0).T

    def strided8(ref, blk):
        return ref[pl.ds((blk // 8) * 256 + blk % 8, 32, stride=8), :]

    for load in loads[:8]:
        load.wait()

    def prep_own(bs):
        for j, blk in enumerate(bs):
            interleave(j, strided8(diag_v, blk), strided8(smooth_v, blk))
        for j, blk in enumerate(bs):
            settle(j, blk, 256)

    loop(prep_own, NB, UN)

    zero2 = jnp.zeros((2, 128), F32)

    def first_smooth(ts):
        for t in ts:
            tile = rhs_v[:, pl.ds(pl.multiple_of(t * 128, 128), 128)]
            tile = jnp.concatenate([tile, zero2], axis=0)
            other = swap(tile)
            for blk, both in ((2 * t, pick(tile, other)), (2 * t + 1, pick(other, tile))):
                b_f[blk] = both
                step = apply_s(both, blk, R)
                x_f[blk] = step
                put(fields, 0, blk, step, R)

    loop(first_smooth, TILES, 16)

    pl.semaphore_wait(barrier, len(greeted))
    halo1 = send_halo(0, x_f, snd, rcv, 0)

    loads[8].wait()

    def prep_off(bs):
        for j, blk in enumerate(bs):
            parts = [off_v[pl.ds(blk * 128 + k, 32, stride=4), :] for k in range(KB)]
            interleave(2 * j, parts[0], parts[1])
            interleave(2 * j + 1, parts[2], parts[3])
        for j, blk in enumerate(bs):
            settle(2 * j, blk, 0)
            settle(2 * j + 1, blk, 128)

    loop(prep_off, NB, UN)

    take_halo(halo1, fields, 0, rcv, 0, R)

    def second_a(bs):
        out = [b_f[blk] - apply_a(fields, 0, blk, R) for blk in bs]
        for blk, resid in zip(bs, out):
            r_f[blk] = resid

    loop(second_a, NB, UN)

    def second_s(bs):
        done = [x_f[blk] + apply_s(r_f[blk], blk, R) for blk in bs]
        for blk, both in zip(bs, done):
            put(fields, 1, blk, both, R)
            w_f[blk] = both

    loop(second_s, NB, UN)
    halo2 = send_halo(1, w_f, snd, rcv, 1)

    inv = 1.0 / cdiag_v[...]
    gain = cgain_v[...] * inv
    weight = cweight_v[...]
    own_hot = (
        lax.broadcasted_iota(jnp.int32, (NOWN, NA), 0) == owner_v[...]
    ).astype(F32)
    rows_a = lax.broadcasted_iota(jnp.int32, (NA, 256), 0)

    def build_hot(us):
        for u in us:
            line = [agg_v[pl.ds(2 * u + i, 1), :] for i in range(2)]
            one = (rows_a == jnp.concatenate(line, axis=1)).astype(F32).astype(BF16)
            hot[u] = one
            hot_t[u] = one.T

    loop(build_hot, PAIRS, 4)

    g_hi, g_lo = split(own_hot * gain)
    g_lhs = jnp.concatenate([g_hi, g_lo], axis=0)

    def build_pg(us):
        for u in us:
            both = dot_nn(g_lhs, hot[u])
            both = both[:NOWN] + both[NOWN:]
            for i in range(2):
                tile = both[:, 128 * i : 128 * i + 128]
                other = swap(tile)
                for blk, dup in (
                    (4 * u + 2 * i, pick(tile, other)),
                    (4 * u + 2 * i + 1, pick(other, tile)),
                ):
                    e_f[blk] = dup
                    put(owner_fields, 0, blk, dup, NOWN)

    loop(build_pg, PAIRS, 4)
    halo_e1 = send_halo(4, e_f, snd_e, rcv_e, 0)
    take_halo(halo2, fields, 1, rcv, 1, R)

    def triple(tile):
        hi, lo = split(tile)
        return jnp.concatenate([hi, hi, lo], axis=0)

    def resid_all(bs):
        out = [b_f[blk] - apply_a(fields, 1, blk, R) for blk in bs]
        for blk, resid in zip(bs, out):
            r_f[blk] = resid

    loop(resid_all, NB, UN)

    def restrict(i, acc):
        for j in range(8):
            blk = (i * 8 + j) * 4
            tiles = [pick(r_f[blk + 2 * h], r_f[blk + 2 * h + 1]) for h in range(2)]
            hi, lo = split(jnp.concatenate(tiles, axis=1))
            acc = acc + dot_nn(jnp.concatenate([hi, lo], axis=0), hot_t[i * 8 + j])
        return acc

    acc = lax.fori_loop(0, PAIRS // 8, restrict, jnp.zeros((2 * R, NA), F32))
    coarse = (acc[:R] + acc[R:]) * inv
    e_hi, e_lo = split(coarse)
    e_lhs = jnp.concatenate([e_hi, e_lo], axis=0)

    def prolong(us):
        for u in us:
            both = dot_nn(e_lhs, hot[u])
            both = both[:R] + both[R:]
            for i in range(2):
                tile = both[:, 128 * i : 128 * i + 128]
                other = swap(tile)
                for blk, dup in (
                    (4 * u + 2 * i, pick(tile, other)),
                    (4 * u + 2 * i + 1, pick(other, tile)),
                ):
                    b_f[blk] = dup
                    put(fields, 0, blk, dup, R)

    loop(prolong, PAIRS, 4)
    halo3 = send_halo(2, b_f, snd, rcv, 2)

    row = lax.broadcasted_iota(jnp.int32, (R, NA), 0)
    weighted = jnp.where(row == TERMS, gain, coarse) * weight
    part = dot_nt(own_hot, weighted, lax.Precision.HIGHEST)
    sum_a[0] = jnp.concatenate([part, jnp.zeros((NOWN, 128 - R), F32)], axis=1)
    copies_a = [
        pltpu.make_async_remote_copy(
            src_ref=sum_a.at[0],
            dst_ref=sum_a.at[j + 1],
            send_sem=a_send.at[0],
            recv_sem=a_recv.at[0],
            device_id=peer,
            device_id_type=MESH,
        )
        for j, peer in enumerate(peers_a)
    ]
    landed_a = sum_a.at[1 : len(peers_a) + 1]
    for copy in copies_a:
        copy.start()

    take_halo(halo_e1, owner_fields, 0, rcv_e, 0, NOWN)

    def owner_a(bs):
        out = [-apply_a(owner_fields, 0, blk, NOWN) for blk in bs]
        for blk, resid in zip(bs, out):
            g_f[blk] = resid

    loop(owner_a, NB, UN)

    def owner_s(bs):
        done = [e_f[blk] + apply_s(g_f[blk], blk, NOWN) for blk in bs]
        for blk, both in zip(bs, done):
            put(owner_fields, 1, blk, both, NOWN)
            g_f[blk] = both
        for i in range(0, len(bs), 2):
            c_x[bs[i] // 2] = triple(pick(done[i], done[i + 1]))

    loop(owner_s, NB, UN)
    halo_e2 = send_halo(5, g_f, snd_e, rcv_e, 1)

    pltpu.make_async_copy(landed_a, landed_a, a_recv.at[0]).wait()
    sum_b[0] = jnp.sum(sum_a[...], axis=0)
    copies_b = [
        pltpu.make_async_remote_copy(
            src_ref=sum_b.at[0],
            dst_ref=sum_b.at[j + 1],
            send_sem=b_send.at[0],
            recv_sem=b_recv.at[0],
            device_id=peer,
            device_id_type=MESH,
        )
        for j, peer in enumerate(peers_b)
    ]
    landed_b = sum_b.at[1 : len(peers_b) + 1]
    for copy in copies_b:
        copy.start()
    take_halo(halo3, fields, 0, rcv, 2, R)

    def third_a(bs):
        out = [r_f[blk] - apply_a(fields, 0, blk, R) for blk in bs]
        for blk, resid in zip(bs, out):
            x_f[blk] = resid

    loop(third_a, NB, UN)

    def third_s(bs):
        done = [apply_s(x_f[blk], blk, R) for blk in bs]
        for blk, step in zip(bs, done):
            put(fields, 1, blk, step, R)
            r_f[blk] = step

    loop(third_s, NB, UN)
    halo4 = send_halo(3, r_f, snd, rcv, 3)

    take_halo(halo_e2, owner_fields, 1, rcv_e, 1, NOWN)

    def owner_r(bs):
        out = [-apply_a(owner_fields, 1, blk, NOWN) for blk in bs]
        for i in range(0, len(bs), 2):
            c_r[bs[i] // 2] = triple(pick(out[i], out[i + 1]))

    loop(owner_r, NB, UN)

    if peers_b:
        pltpu.make_async_copy(landed_b, landed_b, b_recv.at[0]).wait()
    total = jnp.sum(sum_b[...], axis=0)[:, 0:R]
    total = total * (1.0 + total[:, TERMS : TERMS + 1])
    keep = lax.broadcasted_iota(jnp.int32, (NOWN, R), 1) < TERMS
    s_hi, s_lo = split(jnp.where(keep, total, 0.0).T)
    s_lhs = jnp.concatenate([s_hi, s_lo, s_hi], axis=1)

    def finish(ts):
        for t in ts:
            parts = [b_f[blk] + r_f[blk] + w_f[blk] for blk in (2 * t, 2 * t + 1)]
            tile = pick(parts[0], parts[1]) + dot_nn(s_lhs, c_x[t])
            sol_v[:, pl.ds(pl.multiple_of(t * 128, 128), 128)] = tile[:TERMS]

    loop(finish, TILES, 8)
    store = pltpu.make_async_copy(sol_v, out_hbm, load_sem.at[0])
    store.start()

    take_halo(halo4, fields, 1, rcv, 3, R)

    def final(i, acc):
        for j in range(16):
            t = i * 16 + j
            parts = [x_f[blk] - apply_a(fields, 1, blk, R) for blk in (2 * t, 2 * t + 1)]
            tile = pick(parts[0], parts[1]) + dot_nn(s_lhs, c_r[t])
            acc = acc + tile * tile
        return acc

    acc = lax.fori_loop(0, TILES // 16, final, jnp.zeros((R, 128), F32))

    def right_norm(i, acc):
        tile = rhs_v[:, pl.ds(pl.multiple_of(i * 128, 128), 128)]
        return acc + tile * tile

    acc_b = lax.fori_loop(0, TILES, right_norm, jnp.zeros((TERMS, 128), F32))
    sum_f = jnp.sum(acc, axis=0, keepdims=True)
    sum_r = jnp.sum(acc_b, axis=0, keepdims=True)
    norm_v[0, 0] = pick(sum_f + swap(sum_f), sum_r + swap(sum_r))
    norm_copies = []
    for g, peers in enumerate(norm_groups):
        if g:
            norm_v[g, 0] = jnp.sum(norm_v[g - 1, 0 : len(norm_groups[g - 1]) + 1], axis=0)
        if not peers:
            continue
        copies = [
            pltpu.make_async_remote_copy(
                src_ref=norm_v.at[g, 0],
                dst_ref=norm_v.at[g, j + 1],
                send_sem=n_send.at[g],
                recv_sem=n_recv.at[g],
                device_id=peer,
                device_id_type=MESH,
            )
            for j, peer in enumerate(peers)
        ]
        for copy in copies:
            copy.start()
        if g == 0:
            for sent in (halo1, halo2, halo3, halo4, halo_e1, halo_e2):
                for copy in sent:
                    copy.wait_send()
            pltpu.make_async_copy(landed_a, landed_a, a_send.at[0]).wait()
            if peers_b:
                pltpu.make_async_copy(landed_b, landed_b, b_send.at[0]).wait()
        landed = norm_v.at[g, 1 : len(peers) + 1]
        pltpu.make_async_copy(landed, landed, n_recv.at[g]).wait()
        norm_copies.append((g, landed))
    last = len(norm_groups) - 1
    sums = jnp.sum(norm_v[last, 0 : len(norm_groups[last]) + 1], axis=0)
    sum_f = jnp.sum(jnp.where(low, sums, 0.0), axis=1, keepdims=True)
    sum_r = jnp.sum(jnp.where(low, 0.0, sums), axis=1, keepdims=True)
    ratio_ref[...] = jnp.sqrt(sum_f / (sum_r + 1e-6))
    for g, landed in norm_copies:
        pltpu.make_async_copy(landed, landed, n_send.at[g]).wait()

    store.wait()


def on_device(
    zs,
    xs,
    right_side,
    diag_blocks,
    off_blocks,
    smoother,
    col_index,
    send_list,
    agg_map,
    owner_map,
    coarse_diag,
    coarse_weight,
    coarse_gain,
):
    def rows_of(v):
        return v.reshape(8, 8, 32, 128).transpose(0, 2, 1, 3).reshape(NB * 32, 128)

    off = off_blocks.reshape(NB, KB, 32, 128).transpose(0, 2, 1, 3).reshape(NB * KB * 32, 128)
    hbm = pl.BlockSpec(memory_space=pl.ANY)
    smem = pl.BlockSpec(memory_space=pltpu.SMEM)
    dma = pltpu.SemaphoreType.DMA
    scratch = [
        pltpu.VMEM((TERMS, NB * 64), F32),
        pltpu.VMEM((NB * 32, 128), F32),
        pltpu.VMEM((NB * KB * 32, 128), F32),
        pltpu.VMEM((NB * 32, 128), F32),
        pltpu.VMEM((TILES, 128), jnp.int32),
        pltpu.VMEM((1, NA), jnp.int32),
        pltpu.VMEM((1, NA), F32),
        pltpu.VMEM((1, NA), F32),
        pltpu.VMEM((1, NA), F32),
        pltpu.VMEM((NB, 384, 128), BF16),
        pltpu.VMEM((2, NB + 2 * H, 2, 2 * R, 128), BF16),
        pltpu.VMEM((2, NB + 2 * H, 2, 2 * NOWN, 128), BF16),
        pltpu.VMEM((PAIRS, NA, 256), BF16),
        pltpu.VMEM((PAIRS, 256, NA), BF16),
        pltpu.VMEM((NB, R, 128), F32),
        pltpu.VMEM((NB, NOWN, 128), F32),
        pltpu.VMEM((NB, NOWN, 128), F32),
        pltpu.VMEM((NB, R, 128), F32),
        pltpu.VMEM((NB, R, 128), F32),
        pltpu.VMEM((NB, R, 128), F32),
        pltpu.VMEM((TILES, 3 * NOWN, 128), BF16),
        pltpu.VMEM((TILES, 3 * NOWN, 128), BF16),
        pltpu.VMEM((2 * UN, 64, 128), F32),
        pltpu.VMEM((TERMS, NB * 64), F32),
        pltpu.VMEM((4, 2, H // 2, R, 128), F32),
        pltpu.VMEM((4, 2, H // 2, R, 128), F32),
        pltpu.VMEM((2, 2, H // 2, NOWN, 128), F32),
        pltpu.VMEM((2, 2, H // 2, NOWN, 128), F32),
        pltpu.VMEM((YC, NOWN, 128), F32),
        pltpu.VMEM((zs, NOWN, 128), F32),
        pltpu.VMEM((2, 16, 1, 128), F32),
        dma((9,)),
        dma((6, 2)),
        dma((6, 2)),
        dma((1,)),
        dma((1,)),
        dma((1,)),
        dma((1,)),
        dma((2,)),
        dma((2,)),
    ]
    out, ratio = pl.pallas_call(
        functools.partial(kernel, zs, xs),
        out_shape=(
            jax.ShapeDtypeStruct((TERMS, NB * 64), F32),
            jax.ShapeDtypeStruct((1, 1), F32),
        ),
        in_specs=[smem, smem] + [hbm] * 9,
        out_specs=(hbm, pl.BlockSpec(memory_space=pltpu.VMEM)),
        scratch_shapes=scratch,
        compiler_params=pltpu.CompilerParams(
            collective_id=0, has_side_effects=True, vmem_limit_bytes=56 * 1024 * 1024
        ),
    )(
        col_index.T,
        send_list,
        right_side,
        rows_of(diag_blocks),
        off,
        rows_of(smoother),
        agg_map.reshape(TILES, 128),
        owner_map.reshape(1, NA),
        coarse_diag.reshape(1, NA),
        coarse_weight.reshape(1, NA),
        coarse_gain.reshape(1, NA),
    )
    return out, ratio.reshape(())


def solution(mesh):
    placed = (
        P("chaos", "nodes"),
        P("nodes", None),
        P("nodes", None, None),
        P("nodes", None),
        P("nodes", None),
        P("nodes"),
        P("nodes"),
        P("nodes", None),
        P("nodes"),
        P("nodes"),
        P("nodes"),
    )
    return jax.shard_map(
        functools.partial(on_device, mesh.shape["nodes"] // YC, mesh.shape["chaos"]),
        mesh=mesh,
        in_specs=placed,
        out_specs=(P("chaos", "nodes"), P()),
        check_vma=False,
    )
```

time: 58.2 us -> 54.3 us (0.933)
  Pallas kernels: 53.8 us -> 49.9 us
    pallas_call x1, Pallas kernels: 53.8 us -> 49.9 us  [on_device(): pl.pallas_call(functools.partial(kernel, zs, xs), out_shape=(jax.ShapeDty...]
where the time goes in v3:
time: 54.3 us; the launch traced here: 54.1 us
  Pallas kernels  49.9 us (92%)
  between operations  2.34 us (4%)
  local copies, waits for them, and re-layouts  1.87 us (3%)
    pallas_call x1, Pallas kernels, on_device(): pl.pallas_call(functools.partial(kernel, zs, xs), out_shape=(jax.ShapeDty...  49.9 us
    unnamed x1, local copies, waits for them, and re-layouts  1.87 us

profile of v3, /device:TPU:1, one launch (start us, length us, event | category | flops | bytes accessed | tf_op | source)
XLA Modules:
  0.0 54.1 jit_solution(505713733802420168)
XLA Ops:
  0.6 49.9 %shard_map.122 = (f32[30,4096]{1,0:T(8,128)}, f32[1,1]{1,0:T(1,128)}) custom-call(s32[4,64]{1,0:T(4,128)} %bitcast.26, s32[16]{0:T(128)} %send_list.1, f32[30,4096]{1,0:T(8,128)} %rhs_hbm.1, f32[2048,128]{1,0:T(8,128)} %bitcast.23, f32[8192,128]{1,0:T(8,128)} %bitcast.22, f32[2048,128]{1,0:T(8,128)} %bitcast.24, s32[32,128]{1,0:T(8,128)} %bitcast.25, ...), custom_call_target="tpu_custom_call" | custom-call | tf_op jit(solution)/shard_map/pallas_call | solution.py:614
  50.6 1.9 %copy.16 = f32[30,4096]{1,0:T(8,128)} copy(f32[30,4096]{1,0:T(8,128)} %get-tuple-element.8) | data formatting | bytes 983040

commit v4 on v3

--- a/solution.py
+++ b/solution.py
@@ -124,10 +124,10 @@
                 (cdiag_hbm, cdiag_v),
                 (cweight_hbm, cweight_v),
                 (cgain_hbm, cgain_v),
-                (smooth_hbm, smooth_v),
-                (diag_hbm, diag_v),
+                (smooth_hbm, smooth_v.at[0 : NB * 32]),
+                (diag_hbm, diag_v.at[0 : NB * 32]),
                 (rhs_hbm, rhs_v),
-                (off_hbm, off_v),
+                (off_hbm, off_v.at[0 : NB * KB * 32]),
             ]
         )
     ]
@@ -242,7 +242,7 @@
         tmp[j, pl.ds(1, 32, stride=2), :] = pick(a, second)
 
     def settle(j, blk, at):
-        hi, lo = split(tmp[j])
+        hi, lo = split(tmp[j, 0:64])
         mats[blk, at : at + 128, :] = jnp.concatenate([hi, lo], axis=0).T
 
     def strided8(ref, blk):
@@ -571,9 +571,9 @@
     dma = pltpu.SemaphoreType.DMA
     scratch = [
         pltpu.VMEM((TERMS, NB * 64), F32),
-        pltpu.VMEM((NB * 32, 128), F32),
-        pltpu.VMEM((NB * KB * 32, 128), F32),
-        pltpu.VMEM((NB * 32, 128), F32),
+        pltpu.VMEM((NB * 32 + 8, 128), F32),
+        pltpu.VMEM((NB * KB * 32 + 8, 128), F32),
+        pltpu.VMEM((NB * 32 + 8, 128), F32),
         pltpu.VMEM((TILES, 128), jnp.int32),
         pltpu.VMEM((1, NA), jnp.int32),
         pltpu.VMEM((1, NA), F32),
@@ -592,7 +592,7 @@
         pltpu.VMEM((NB, R, 128), F32),
         pltpu.VMEM((TILES, 3 * NOWN, 128), BF16),
         pltpu.VMEM((TILES, 3 * NOWN, 128), BF16),
-        pltpu.VMEM((2 * UN, 64, 128), F32),
+        pltpu.VMEM((2 * UN, 72, 128), F32),
         pltpu.VMEM((TERMS, NB * 64), F32),
         pltpu.VMEM((4, 2, H // 2, R, 128), F32),
         pltpu.VMEM((4, 2, H // 2, R, 128), F32),

time: 54.3 us -> 54.3 us (level)
  no operation moved by 1% of the time
where the time goes in v4:
time: 54.3 us; the launch traced here: 54.1 us
  Pallas kernels  49.9 us (92%)
  between operations  2.34 us (4%)
  local copies, waits for them, and re-layouts  1.87 us (3%)
    pallas_call x1, Pallas kernels, on_device(): pl.pallas_call(functools.partial(kernel, zs, xs), out_shape=(jax.ShapeDty...  49.9 us
    unnamed x1, local copies, waits for them, and re-layouts  1.87 us

profile of v4, /device:TPU:1, one launch (start us, length us, event | category | flops | bytes accessed | tf_op | source)
XLA Modules:
  0.0 54.1 jit_solution(3634915799563537587)
XLA Ops:
  0.6 49.9 %shard_map.122 = (f32[30,4096]{1,0:T(8,128)}, f32[1,1]{1,0:T(1,128)}) custom-call(s32[4,64]{1,0:T(4,128)} %bitcast.26, s32[16]{0:T(128)} %send_list.1, f32[30,4096]{1,0:T(8,128)} %rhs_hbm.1, f32[2048,128]{1,0:T(8,128)} %bitcast.23, f32[8192,128]{1,0:T(8,128)} %bitcast.22, f32[2048,128]{1,0:T(8,128)} %bitcast.24, s32[32,128]{1,0:T(8,128)} %bitcast.25, ...), custom_call_target="tpu_custom_call" | custom-call | tf_op jit(solution)/shard_map/pallas_call | solution.py:614
  50.5 1.9 %copy.16 = f32[30,4096]{1,0:T(8,128)} copy(f32[30,4096]{1,0:T(8,128)} %get-tuple-element.8) | data formatting | bytes 983040
